TPU v7x, 128 devices: a whole 4x4x4 slice. The times are simulated.
128 devices in a mesh: sec: 8 (over x, core), op: 16 (over y, z).
Axes of the slice: x: 4, y: 4, z: 4, core: 2. Of those that a mesh axis runs over, the one named last changes fastest.
Arguments:
- psi: bfloat16 [8192, 256], P(('sec', 'op')), may hold values from -6 to 6
- left_env: bfloat16 [384, 32, 256, 256], P('op', 'sec'), may hold values from -0.01953125 to 0.01953125
- right_env: bfloat16 [384, 32, 256, 256], P('op', 'sec'), may hold values from -0.375 to 0.375
- term_src: int32 [384, 32], P('op', 'sec'), may hold values from 0 to 31, as said below
- block_dims: int32 [2, 32], replicated, may hold values from 64 to 256, as said below
Outputs:
- sigma: bfloat16 [8192, 256], P(('sec', 'op'))
Inputs may be any that keep to these rules, and one draw needn't show every extreme that they name: |term_src[t, k] - k| <= 2 for every t and k, and term_src[t, k] = k + 2 for some t and k. `block_dims`: every entry is a multiple of 4; 256 is reached in each row.
All inputs are finite; a program needn't handle non-finite values.
Results may differ from a plain program's by a relative error of at most 0.0049.
Values may be sent and summed in bfloat16 or wider, within the bound.
A program may use at most 128 MiB of HBM per device.

v0:
```python
import jax
import jax.numpy as jnp
from jax import lax
from jax.sharding import PartitionSpec as P


def padded(cells, sides, width):
    for axis, dim in sides:
        count = lax.axis_size(axis)
        ends = count - 1
        head = lax.slice_in_dim(cells, 0, width, axis=dim)
        tail = lax.slice_in_dim(cells, cells.shape[dim] - width, cells.shape[dim], axis=dim)
        cells = jnp.concatenate(
            [
                lax.ppermute(tail, axis, [(i, (i + 1) % count) for i in range(ends)]),
                cells,
                lax.ppermute(head, axis, [((i + 1) % count, i) for i in range(ends)]),
            ],
            axis=dim,
        )
    return cells


def lookup_dims(block_ids, block_dims):
    count = block_dims.shape[1]
    every_id = jnp.arange(count, dtype=jnp.int32)
    match = block_ids[..., None] == every_id
    rows_used = jnp.sum(jnp.where(match, block_dims[0], 0), axis=-1)
    cols_used = jnp.sum(jnp.where(match, block_dims[1], 0), axis=-1)
    return (rows_used, cols_used)


def shards(psi, left_env, right_env, term_src, block_dims):
    side = psi.shape[1]
    per_sec = left_env.shape[1]
    local_rows = psi.shape[0]
    group_size = lax.axis_size("op")
    extended = padded(psi, (("sec", 0),), local_rows)
    gathered = lax.all_gather(extended, "op", axis=0, tiled=True)
    arranged = gathered.reshape(group_size, 3, local_rows, side).transpose(1, 0, 2, 3)
    blocks = arranged.reshape(-1, side, side)
    first_block = lax.axis_index("sec") * per_sec - per_sec
    local_src = term_src - first_block
    selected = jnp.take(blocks, local_src, axis=0)
    places = jnp.arange(side, dtype=jnp.int32)
    rows_used, cols_used = lookup_dims(term_src, block_dims)
    keep = (places[:, None] < rows_used[..., None, None]) & (
        places[None, :] < cols_used[..., None, None]
    )
    masked = jnp.where(keep, selected, jnp.zeros_like(selected))
    half = jnp.einsum(
        "tkij,tkjl->tkil", masked, right_env, preferred_element_type=jnp.float32
    ).astype(jnp.bfloat16)
    partial_value = jnp.einsum("tkij,tkjl->kil", left_env, half, preferred_element_type=jnp.float32)
    partial_value = partial_value.reshape(per_sec * side, side)
    summed = lax.psum_scatter(partial_value, "op", scatter_dimension=0, tiled=True)
    row_start = (lax.axis_index("sec") * group_size + lax.axis_index("op")) * local_rows
    global_rows = row_start + jnp.arange(local_rows, dtype=jnp.int32)
    out_blocks = global_rows // side
    inner_rows = global_rows % side
    out_rows_used, out_cols_used = lookup_dims(out_blocks, block_dims)
    out_keep = (inner_rows < out_rows_used)[:, None] & (places[None, :] < out_cols_used[:, None])
    return jnp.where(out_keep, summed, jnp.zeros_like(summed)).astype(jnp.bfloat16)


def solution(mesh):
    placed = (
        P(("sec", "op"), None),
        P("op", "sec", None, None),
        P("op", "sec", None, None),
        P("op", "sec"),
        P(),
    )
    return jax.shard_map(
        shards, mesh=mesh, in_specs=placed, out_specs=P(("sec", "op"), None), check_vma=False
    )
```

profile of v0, /device:TPU:0, one launch (start us, length us, event | category | flops | bytes accessed | tf_op | source)
XLA Modules:
  0.0 178.6 jit_solution(1798577908962675282)
XLA Ops:
  6.5 0.0 all-gather.2.cloned.1.call-start
  6.5 1.3 collective-permute-start
  7.8 1.3 collective-permute-start.1
  9.1 0.0 collective-permute-done
  9.1 3.8 %collective-permute-done.1 = bf16[64,256]{1,0:T(8,128)(2,1)S(1)} collective-permute-done((bf16[64,256]{1,0:T(8,128)(2,1)}, bf16[64,256]{1,0:T(8,128)(2,1)S(1)}, u32[]{:S(2)}, u32[]{:S(2)}) %collective-permute-start.1) | collective-permute-done | bytes 32800 | tf_op jit(solution)/shard_map/ppermute | solution.py:17
  12.9 1.4 pad_maximum_fusion
  14.3 0.0 all-gather.2.cloned.1.call-update
  14.4 0.0 reduce-scatter.2.cloned.1.call-start
  14.4 0.7 compare_and_fusion
  15.1 0.1 copy.21
  15.2 0.1 reshape.72
  15.3 0.8 slice_bitcast_fusion
  16.1 1.0 select_reduce_fusion.1
  17.0 0.1 iota_compare_fusion
  17.1 45.8 %all-gather.2.cloned.1.call-done = bf16[3072,256]{1,0:T(8,128)(2,1)} async-done(((bf16[192,256]{1,0:T(8,128)(2,1)}), bf16[3072,256]{1,0:T(8,128)(2,1)}) %all-gather.2.cloned.1.call-update) | async-done | bytes 1572880 | tf_op jit(solution)/shard_map/all_gather | solution.py:39
  63.0 1.5 copy.20
  64.5 6.7 %gather_fusion = bf16[96,256,256]{2,1,0:T(8,128)(2,1)} fusion(bf16[12,256,256]{2,1,0:T(8,128)(2,1)S(1)} %bitcast.16, s32[1024]{0:T(1024)S(1)} %pad_clamp_fusion), kind=kCustom, calls=%fused_computation | custom fusion | bytes 25166208 | tf_op jit(solution)/shard_map/jit(_take)/gather | solution.py:44
  71.2 13.9 %fusion.26 = bf16[24,4,256,256]{3,2,0,1:T(8,128)(2,1)} fusion(bf16[24,4,256,256]{3,2,1,0:T(8,128)(2,1)} %param.7, bf16[24,4,256,256]{3,2,1,0:T(8,128)(2,1)} %bitcast.17, pred[24,4]{0,1:T(4,128)(4,1)S(1)} %get-tuple-element.9, pred[24,4,256]{2,0,1:T(8,128)(4,1)S(1)} %get-tuple-element.13, pred[24,4,256]{2,0,1:T(8,128)(4,1)S(1)} %get-tuple-element.14), kind=kOutput, calls=%fused_computation.7.clone.1 | convolution fusion | flops 3246391296 | bytes 37797984 | tf_op jit(solution)/shard_map/tkij,tkjl->tkil/dot_general | solution.py:51
  85.1 12.6 %fusion.1 = f32[4,256,256,1]{1,2,3,0:T(8,128)} fusion(bf16[24,4,256,256]{3,2,1,0:T(8,128)(2,1)} %param.6, bf16[24,4,256,256]{3,2,0,1:T(8,128)(2,1)} %fusion.26), kind=kOutput, calls=%fused_computation.3 | convolution fusion | flops 3221225472 | bytes 26214400 | tf_op jit(solution)/shard_map/tkij,tkjl->kil/dot_general | solution.py:54
  97.7 0.0 reduce-scatter.2.cloned.1.call-update
  97.8 0.1 select_reduce_fusion.3
  97.9 72.4 %reduce-scatter.2.cloned.1.call-done = f32[64,256]{1,0:T(8,128)} async-done(((f32[1024,256]{1,0:T(8,128)}), f32[64,256]{1,0:T(8,128)}) %reduce-scatter.2.cloned.1.call-update) | async-done | bytes 65552 | tf_op jit(solution)/shard_map/reduce_scatter | solution.py:56
  170.2 1.5 select_convert_fusion
  (3 shorter events, 0.0 us)
Async XLA Ops:
  6.5 56.4 %all-gather.2.cloned.1.call-start = ((), (), s32[]{:S(2)}) async-start(), calls=%async_computation.1 | async-start | bytes 1671168 | tf_op jit(solution)/shard_map/all_gather | solution.py:39
  6.5 2.6 %collective-permute-start = (bf16[64,256]{1,0:T(8,128)(2,1)}, bf16[64,256]{1,0:T(8,128)(2,1)S(1)}, u32[]{:S(2)}, u32[]{:S(2)}) collective-permute-start(bf16[64,256]{1,0:T(8,128)(2,1)} %param.5), channel_id=1, source_target_pairs={{0,16},{16,32},{32,48},{48,64},{64,80},{80,96},{96,112},{1,17},{17... | collective-permute-start | bytes 98312 | tf_op jit(solution)/shard_map/ppermute | solution.py:15
  7.8 5.1 %collective-permute-start.1 = (bf16[64,256]{1,0:T(8,128)(2,1)}, bf16[64,256]{1,0:T(8,128)(2,1)S(1)}, u32[]{:S(2)}, u32[]{:S(2)}) collective-permute-start(bf16[64,256]{1,0:T(8,128)(2,1)} %param.5), channel_id=1, source_target_pairs={{16,0},{32,16},{48,32},{64,48},{80,64},{96,80},{112,96},{17,1},{33... | collective-permute-start | bytes 98312 | tf_op jit(solution)/shard_map/ppermute | solution.py:17
  14.4 155.9 %reduce-scatter.2.cloned.1.call-start = ((), (), s32[]{:S(2)}) async-start(), calls=%async_computation.2 | async-start | bytes 1114112 | tf_op jit(solution)/shard_map/reduce_scatter | solution.py:56
Sparse Core Ops, SparseCore 0:
  14.5 48.4 all-gather.1
  97.8 72.3 reduce-scatter.1
where the time goes:
time: 179 us
  waiting for transfers between devices  122 us (68%)
  matrix products  26.5 us (15%)
  between operations  13.5 us (8%)
  local copies, waits for them, and re-layouts  9.16 us (5%)
  other arithmetic  4.82 us (3%)
  starting transfers between devices  2.62 us (1%)
    reduce_scatter x1, waiting for transfers between devices, shards(): lax.psum_scatter(partial_value, 'op', scatter_dimension=0, tiled=True)  72.4 us
    all_gather x1, waiting for transfers between devices, shards(): gathered = lax.all_gather(extended, 'op', axis=0, tiled=True)  45.8 us
    dot_general x1, matrix products, shards(): jnp.einsum('tkij,tkjl->tkil', masked, right_env, preferred_element_type=j...  13.9 us
    dot_general x1, matrix products, shards(): jnp.einsum('tkij,tkjl->kil', left_env, half, preferred_element_type=jnp.f...  12.6 us
    gather x1, local copies, waits for them, and re-layouts, shards(): selected = jnp.take(blocks, local_src, axis=0)  6.71 us
    ppermute x1, waiting for transfers between devices, padded(): lax.ppermute(head, axis, [((i + 1) % count, i) for i in range(ends)])  3.81 us
  transfers between devices with their start and end apart: 4, of which 3 were waited for; matrix products, arithmetic and copies ran while one was open for 2% of the time, Pallas kernels for 0%

commit v1 on v0

--- a/solution.py
+++ b/solution.py
@@ -2,6 +2,27 @@
 import jax.numpy as jnp
 from jax import lax
 from jax.sharding import PartitionSpec as P
+
+
+def collect(array, axis, dim):
+    peers, mine, span = (lax.axis_size(axis), lax.axis_index(axis), array.shape[dim])
+    forward = [(i, (i + 1) % peers) for i in range(peers)]
+    downward = [(i, (i - 1) % peers) for i in range(peers)]
+    filled = jnp.zeros((*array.shape[:dim], peers * span, *array.shape[dim + 1 :]), array.dtype)
+    filled = lax.dynamic_update_slice_in_dim(filled, array, mine * span, axis=dim)
+    from_left = from_right = array
+    halfway = peers // 2
+    for step in range(1, halfway + 1):
+        from_left = lax.ppermute(from_left, axis, forward)
+        filled = lax.dynamic_update_slice_in_dim(
+            filled, from_left, (mine - step) % peers * span, axis=dim
+        )
+        if step < peers - halfway:
+            from_right = lax.ppermute(from_right, axis, downward)
+            filled = lax.dynamic_update_slice_in_dim(
+                filled, from_right, (mine + step) % peers * span, axis=dim
+            )
+    return filled
 
 
 def padded(cells, sides, width):
@@ -36,7 +57,7 @@
     local_rows = psi.shape[0]
     group_size = lax.axis_size("op")
     extended = padded(psi, (("sec", 0),), local_rows)
-    gathered = lax.all_gather(extended, "op", axis=0, tiled=True)
+    gathered = collect(extended, "op", 0)
     arranged = gathered.reshape(group_size, 3, local_rows, side).transpose(1, 0, 2, 3)
     blocks = arranged.reshape(-1, side, side)
     first_block = lax.axis_index("sec") * per_sec - per_sec

time: 179 us -> 199 us (1.11)
  starting transfers between devices: 2.62 us -> 44.2 us
  waiting for transfers between devices: 122 us -> 101 us
    all_gather x1 -> x0, waiting for transfers between devices: 45.8 us -> none  [shards(): gathered = lax.all_gather(extended, 'op', axis=0, tiled=True)]
    ppermute x0 -> x15, starting transfers between devices: none -> 41.6 us  [the longest x7 41.6 us: collect(): from_right = lax.ppermute(from_right, axis, downward)]
    ppermute x0 -> x15, waiting for transfers between devices: none -> 29.8 us  [the longest x8 17.2 us: collect(): from_left = lax.ppermute(from_left, axis, forward)]
    ppermute x1, waiting for transfers between devices: 3.81 us -> 0.01 us  [padded(): lax.ppermute(head, axis, [((i + 1) % count, i) for i in range(ends)])]
  transfers between devices with their start and end apart: 4 -> 18, of which waited for: 3 -> 14; matrix products, arithmetic and copies ran while one was open for 2% -> 2% of each run, Pallas kernels for 0% -> 0%
where the time goes in v1:
time: 199 us; the launch traced here: 198 us
  waiting for transfers between devices  101 us (51%)
  starting transfers between devices  44.2 us (22%)
  matrix products  26.5 us (13%)
  between operations  13.9 us (7%)
  local copies, waits for them, and re-layouts  8.89 us (4%)
  other arithmetic  3.43 us (2%)
    reduce_scatter x1, waiting for transfers between devices, shards(): lax.psum_scatter(partial_value, 'op', scatter_dimension=0, tiled=True)  71.6 us
    ppermute x7, starting transfers between devices, collect(): from_right = lax.ppermute(from_right, axis, downward)  41.6 us
    ppermute x8, waiting for transfers between devices, collect(): from_left = lax.ppermute(from_left, axis, forward)  17.2 us
    dot_general x1, matrix products, shards(): jnp.einsum('tkij,tkjl->tkil', masked, right_env, preferred_element_type=j...  13.9 us
    ppermute x7, waiting for transfers between devices, collect(): from_right = lax.ppermute(from_right, axis, downward)  12.6 us
    dot_general x1, matrix products, shards(): jnp.einsum('tkij,tkjl->kil', left_env, half, preferred_element_type=jnp.f...  12.6 us
    gather x1, local copies, waits for them, and re-layouts, shards(): selected = jnp.take(blocks, local_src, axis=0)  6.72 us
  transfers between devices with their start and end apart: 18, of which 14 were waited for; matrix products, arithmetic and copies ran while one was open for 2% of the time, Pallas kernels for 0%

profile of v1, /device:TPU:0, one launch (start us, length us, event | category | flops | bytes accessed | tf_op | source)
XLA Modules:
  0.0 198.4 jit_solution(15223587420924496442)
XLA Ops:
  6.5 1.3 collective-permute-start
  7.8 1.3 collective-permute-start.1
  9.1 0.8 slice_bitcast_fusion
  9.9 0.7 compare_and_fusion
  10.6 0.1 copy.21
  10.7 0.1 reshape.72
  10.8 1.0 select_reduce_fusion.1
  11.7 0.1 iota_compare_fusion
  12.2 0.0 collective-permute-done
  12.2 0.8 constant_dynamic-update-slice_fusion.1
  12.9 0.0 collective-permute-done.1
  13.0 7.1 %collective-permute-start.3 = (bf16[192,256]{1,0:T(8,128)(2,1)S(1)}, bf16[192,256]{1,0:T(8,128)(2,1)S(1)}, u32[]{:S(2)}, u32[]{:S(2)}) collective-permute-start(bf16[192,256]{1,0:T(8,128)(2,1)S(1)} %constant_dynamic-update-slice_fusion), channel_id=1, source_target_pairs={{0,15},{1,0},{2,1},{3,2},{4,3},{5,4},{6,5},{7,6},{8,7},{9,8},{10,9... | collective-permute-start | bytes 294920 | tf_op jit(solution)/shard_map/ppermute | solution.py:21
  20.0 0.0 collective-permute-start.2
  20.0 0.1 broadcast_in_dim.61
  20.2 2.1 %collective-permute-done.3 = bf16[192,256]{1,0:T(8,128)(2,1)S(1)} collective-permute-done((bf16[192,256]{1,0:T(8,128)(2,1)S(1)}, bf16[192,256]{1,0:T(8,128)(2,1)S(1)}, u32[]{:S(2)}, u32[]{:S(2)}) %collective-permute-start.3) | collective-permute-done | bytes 98336 | tf_op jit(solution)/shard_map/ppermute | solution.py:21
  22.3 5.7 %collective-permute-start.5 = (bf16[192,256]{1,0:T(8,128)(2,1)S(1)}, bf16[192,256]{1,0:T(8,128)(2,1)S(1)}, u32[]{:S(2)}, u32[]{:S(2)}) collective-permute-start(bf16[192,256]{1,0:T(8,128)(2,1)S(1)} %collective-permute-done.3), channel_id=1, source_target_pairs={{0,15},{1,0},{2,1},{3,2},{4,3},{5,4},{6,5},{7,6},{8,7},{9,8},{10,9... | collective-permute-start | bytes 294920 | tf_op jit(solution)/shard_map/ppermute | solution.py:21
  28.0 0.0 collective-permute-done.2
  28.0 0.0 collective-permute-start.4
  28.0 2.9 %collective-permute-done.5 = bf16[192,256]{1,0:T(8,128)(2,1)S(1)} collective-permute-done((bf16[192,256]{1,0:T(8,128)(2,1)S(1)}, bf16[192,256]{1,0:T(8,128)(2,1)S(1)}, u32[]{:S(2)}, u32[]{:S(2)}) %collective-permute-start.5) | collective-permute-done | bytes 98336 | tf_op jit(solution)/shard_map/ppermute | solution.py:21
  30.9 5.8 %collective-permute-start.7 = (bf16[192,256]{1,0:T(8,128)(2,1)S(1)}, bf16[192,256]{1,0:T(8,128)(2,1)S(1)}, u32[]{:S(2)}, u32[]{:S(2)}) collective-permute-start(bf16[192,256]{1,0:T(8,128)(2,1)S(1)} %collective-permute-done.5), channel_id=1, source_target_pairs={{0,15},{1,0},{2,1},{3,2},{4,3},{5,4},{6,5},{7,6},{8,7},{9,8},{10,9... | collective-permute-start | bytes 294920 | tf_op jit(solution)/shard_map/ppermute | solution.py:21
  36.7 0.3 collective-permute-done.4
  37.0 0.0 collective-permute-start.6
  37.0 2.0 %collective-permute-done.7 = bf16[192,256]{1,0:T(8,128)(2,1)S(1)} collective-permute-done((bf16[192,256]{1,0:T(8,128)(2,1)S(1)}, bf16[192,256]{1,0:T(8,128)(2,1)S(1)}, u32[]{:S(2)}, u32[]{:S(2)}) %collective-permute-start.7) | collective-permute-done | bytes 98336 | tf_op jit(solution)/shard_map/ppermute | solution.py:21
  39.0 5.8 %collective-permute-start.9 = (bf16[192,256]{1,0:T(8,128)(2,1)S(1)}, bf16[192,256]{1,0:T(8,128)(2,1)S(1)}, u32[]{:S(2)}, u32[]{:S(2)}) collective-permute-start(bf16[192,256]{1,0:T(8,128)(2,1)S(1)} %collective-permute-done.7), channel_id=1, source_target_pairs={{0,15},{1,0},{2,1},{3,2},{4,3},{5,4},{6,5},{7,6},{8,7},{9,8},{10,9... | collective-permute-start | bytes 294920 | tf_op jit(solution)/shard_map/ppermute | solution.py:21
  44.8 0.3 collective-permute-done.6
  45.1 0.0 collective-permute-start.8
  45.1 1.9 collective-permute-done.9
  47.0 5.7 %collective-permute-start.11 = (bf16[192,256]{1,0:T(8,128)(2,1)S(1)}, bf16[192,256]{1,0:T(8,128)(2,1)S(1)}, u32[]{:S(2)}, u32[]{:S(2)}) collective-permute-start(bf16[192,256]{1,0:T(8,128)(2,1)S(1)} %collective-permute-done.9), channel_id=1, source_target_pairs={{0,15},{1,0},{2,1},{3,2},{4,3},{5,4},{6,5},{7,6},{8,7},{9,8},{10,9... | collective-permute-start | bytes 294920 | tf_op jit(solution)/shard_map/ppermute | solution.py:21
  52.8 0.3 collective-permute-done.8
  53.0 0.0 collective-permute-start.10
  53.1 1.9 collective-permute-done.11
  55.0 5.7 %collective-permute-start.13 = (bf16[192,256]{1,0:T(8,128)(2,1)S(1)}, bf16[192,256]{1,0:T(8,128)(2,1)S(1)}, u32[]{:S(2)}, u32[]{:S(2)}) collective-permute-start(bf16[192,256]{1,0:T(8,128)(2,1)S(1)} %collective-permute-done.11), channel_id=1, source_target_pairs={{0,15},{1,0},{2,1},{3,2},{4,3},{5,4},{6,5},{7,6},{8,7},{9,8},{10,9... | collective-permute-start | bytes 294920 | tf_op jit(solution)/shard_map/ppermute | solution.py:21
  60.7 0.3 collective-permute-done.10
  61.0 0.0 collective-permute-start.12
  61.0 1.9 collective-permute-done.13
  62.9 5.7 %collective-permute-start.15 = (bf16[192,256]{1,0:T(8,128)(2,1)S(1)}, bf16[192,256]{1,0:T(8,128)(2,1)S(1)}, u32[]{:S(2)}, u32[]{:S(2)}) collective-permute-start(bf16[192,256]{1,0:T(8,128)(2,1)S(1)} %collective-permute-done.13), channel_id=1, source_target_pairs={{0,15},{1,0},{2,1},{3,2},{4,3},{5,4},{6,5},{7,6},{8,7},{9,8},{10,9... | collective-permute-start | bytes 294920 | tf_op jit(solution)/shard_map/ppermute | solution.py:21
  68.6 0.3 collective-permute-done.12
  68.9 0.0 collective-permute-start.14
  69.0 7.9 %collective-permute-done.14 = bf16[192,256]{1,0:T(8,128)(2,1)S(1)} collective-permute-done((bf16[192,256]{1,0:T(8,128)(2,1)S(1)}, bf16[192,256]{1,0:T(8,128)(2,1)S(1)}, u32[]{:S(2)}, u32[]{:S(2)}) %collective-permute-start.14) | collective-permute-done | bytes 98336 | tf_op jit(solution)/shard_map/ppermute | solution.py:16
  76.9 7.9 %collective-permute-done.16 = bf16[192,256]{1,0:T(8,128)(2,1)S(1)} collective-permute-done((bf16[192,256]{1,0:T(8,128)(2,1)S(1)}, bf16[192,256]{1,0:T(8,128)(2,1)S(1)}, u32[]{:S(2)}, u32[]{:S(2)}) %collective-permute-start.16) | collective-permute-done | bytes 98336 | tf_op jit(solution)/shard_map/ppermute | solution.py:16
  84.8 0.2 copy.20
  85.0 6.7 %gather_fusion = bf16[96,256,256]{2,1,0:T(8,128)(2,1)} fusion(bf16[12,256,256]{2,1,0:T(8,128)(2,1)S(1)} %bitcast.16, s32[1024]{0:T(1024)S(1)} %pad_clamp_fusion), kind=kCustom, calls=%fused_computation | custom fusion | bytes 25166208 | tf_op jit(solution)/shard_map/jit(_take)/gather | solution.py:65
  91.7 13.9 %fusion.26 = bf16[24,4,256,256]{3,2,0,1:T(8,128)(2,1)} fusion(bf16[24,4,256,256]{3,2,1,0:T(8,128)(2,1)} %param.7, bf16[24,4,256,256]{3,2,1,0:T(8,128)(2,1)} %bitcast.17, pred[24,4]{0,1:T(4,128)(4,1)S(1)} %get-tuple-element.9, pred[24,4,256]{2,0,1:T(8,128)(4,1)S(1)} %get-tuple-element.13, pred[24,4,256]{2,0,1:T(8,128)(4,1)S(1)} %get-tuple-element.14), kind=kOutput, calls=%fused_computation.7.clone.1 | convolution fusion | flops 3246391296 | bytes 37797984 | tf_op jit(solution)/shard_map/tkij,tkjl->tkil/dot_general | solution.py:72
  105.6 12.6 %fusion.1 = f32[4,256,256,1]{1,2,3,0:T(8,128)} fusion(bf16[24,4,256,256]{3,2,1,0:T(8,128)(2,1)} %param.6, bf16[24,4,256,256]{3,2,0,1:T(8,128)(2,1)} %fusion.26), kind=kOutput, calls=%fused_computation.3 | convolution fusion | flops 3221225472 | bytes 26214400 | tf_op jit(solution)/shard_map/tkij,tkjl->kil/dot_general | solution.py:75
  118.2 0.0 reduce-scatter.2.cloned.1.call-update
  118.3 0.1 select_reduce_fusion.3
  118.4 71.6 %reduce-scatter.2.cloned.1.call-done = f32[64,256]{1,0:T(8,128)} async-done(((f32[1024,256]{1,0:T(8,128)}), f32[64,256]{1,0:T(8,128)}) %reduce-scatter.2.cloned.1.call-update) | async-done | bytes 65552 | tf_op jit(solution)/shard_map/reduce_scatter | solution.py:77
  190.0 1.5 select_convert_fusion
  (24 shorter events, 0.2 us)
Async XLA Ops:
  6.5 183.4 %reduce-scatter.2.cloned.1.call-start = ((), (), s32[]{:S(2)}) async-start(), calls=%async_computation.1 | async-start | bytes 1114112 | tf_op jit(solution)/shard_map/reduce_scatter | solution.py:77
  6.5 5.6 %collective-permute-start = (bf16[64,256]{1,0:T(8,128)(2,1)}, bf16[64,256]{1,0:T(8,128)(2,1)S(1)}, u32[]{:S(2)}, u32[]{:S(2)}) collective-permute-start(bf16[64,256]{1,0:T(8,128)(2,1)} %param.5), channel_id=1, source_target_pairs={{0,16},{16,32},{32,48},{48,64},{64,80},{80,96},{96,112},{1,17},{17... | collective-permute-start | bytes 98312 | tf_op jit(solution)/shard_map/ppermute | solution.py:36
  7.8 5.1 %collective-permute-start.1 = (bf16[64,256]{1,0:T(8,128)(2,1)}, bf16[64,256]{1,0:T(8,128)(2,1)S(1)}, u32[]{:S(2)}, u32[]{:S(2)}) collective-permute-start(bf16[64,256]{1,0:T(8,128)(2,1)} %param.5), channel_id=1, source_target_pairs={{16,0},{32,16},{48,32},{64,48},{80,64},{96,80},{112,96},{17,1},{33... | collective-permute-start | bytes 98312 | tf_op jit(solution)/shard_map/ppermute | solution.py:38
  13.0 9.3 %collective-permute-start.3 = (bf16[192,256]{1,0:T(8,128)(2,1)S(1)}, bf16[192,256]{1,0:T(8,128)(2,1)S(1)}, u32[]{:S(2)}, u32[]{:S(2)}) collective-permute-start(bf16[192,256]{1,0:T(8,128)(2,1)S(1)} %constant_dynamic-update-slice_fusion), channel_id=1, source_target_pairs={{0,15},{1,0},{2,1},{3,2},{4,3},{5,4},{6,5},{7,6},{8,7},{9,8},{10,9... | collective-permute-start | bytes 294920 | tf_op jit(solution)/shard_map/ppermute | solution.py:21
  20.0 7.9 %collective-permute-start.2 = (bf16[192,256]{1,0:T(8,128)(2,1)S(1)}, bf16[192,256]{1,0:T(8,128)(2,1)S(1)}, u32[]{:S(2)}, u32[]{:S(2)}) collective-permute-start(bf16[192,256]{1,0:T(8,128)(2,1)S(1)} %constant_dynamic-update-slice_fusion), channel_id=1, source_target_pairs={{0,1},{1,2},{2,3},{3,4},{4,5},{5,6},{6,7},{7,8},{8,9},{9,10},{10,1... | collective-permute-start | bytes 294920 | tf_op jit(solution)/shard_map/ppermute | solution.py:16
  22.3 8.6 %collective-permute-start.5 = (bf16[192,256]{1,0:T(8,128)(2,1)S(1)}, bf16[192,256]{1,0:T(8,128)(2,1)S(1)}, u32[]{:S(2)}, u32[]{:S(2)}) collective-permute-start(bf16[192,256]{1,0:T(8,128)(2,1)S(1)} %collective-permute-done.3), channel_id=1, source_target_pairs={{0,15},{1,0},{2,1},{3,2},{4,3},{5,4},{6,5},{7,6},{8,7},{9,8},{10,9... | collective-permute-start | bytes 294920 | tf_op jit(solution)/shard_map/ppermute | solution.py:21
  28.0 9.0 %collective-permute-start.4 = (bf16[192,256]{1,0:T(8,128)(2,1)S(1)}, bf16[192,256]{1,0:T(8,128)(2,1)S(1)}, u32[]{:S(2)}, u32[]{:S(2)}) collective-permute-start(bf16[192,256]{1,0:T(8,128)(2,1)S(1)} %collective-permute-done.2), channel_id=1, source_target_pairs={{0,1},{1,2},{2,3},{3,4},{4,5},{5,6},{6,7},{7,8},{8,9},{9,10},{10,1... | collective-permute-start | bytes 294920 | tf_op jit(solution)/shard_map/ppermute | solution.py:16
  30.9 8.1 %collective-permute-start.7 = (bf16[192,256]{1,0:T(8,128)(2,1)S(1)}, bf16[192,256]{1,0:T(8,128)(2,1)S(1)}, u32[]{:S(2)}, u32[]{:S(2)}) collective-permute-start(bf16[192,256]{1,0:T(8,128)(2,1)S(1)} %collective-permute-done.5), channel_id=1, source_target_pairs={{0,15},{1,0},{2,1},{3,2},{4,3},{5,4},{6,5},{7,6},{8,7},{9,8},{10,9... | collective-permute-start | bytes 294920 | tf_op jit(solution)/shard_map/ppermute | solution.py:21
  37.0 8.1 %collective-permute-start.6 = (bf16[192,256]{1,0:T(8,128)(2,1)S(1)}, bf16[192,256]{1,0:T(8,128)(2,1)S(1)}, u32[]{:S(2)}, u32[]{:S(2)}) collective-permute-start(bf16[192,256]{1,0:T(8,128)(2,1)S(1)} %collective-permute-done.4), channel_id=1, source_target_pairs={{0,1},{1,2},{2,3},{3,4},{4,5},{5,6},{6,7},{7,8},{8,9},{9,10},{10,1... | collective-permute-start | bytes 294920 | tf_op jit(solution)/shard_map/ppermute | solution.py:16
  39.0 8.0 %collective-permute-start.9 = (bf16[192,256]{1,0:T(8,128)(2,1)S(1)}, bf16[192,256]{1,0:T(8,128)(2,1)S(1)}, u32[]{:S(2)}, u32[]{:S(2)}) collective-permute-start(bf16[192,256]{1,0:T(8,128)(2,1)S(1)} %collective-permute-done.7), channel_id=1, source_target_pairs={{0,15},{1,0},{2,1},{3,2},{4,3},{5,4},{6,5},{7,6},{8,7},{9,8},{10,9... | collective-permute-start | bytes 294920 | tf_op jit(solution)/shard_map/ppermute | solution.py:21
  45.1 7.9 %collective-permute-start.8 = (bf16[192,256]{1,0:T(8,128)(2,1)S(1)}, bf16[192,256]{1,0:T(8,128)(2,1)S(1)}, u32[]{:S(2)}, u32[]{:S(2)}) collective-permute-start(bf16[192,256]{1,0:T(8,128)(2,1)S(1)} %collective-permute-done.6), channel_id=1, source_target_pairs={{0,1},{1,2},{2,3},{3,4},{4,5},{5,6},{6,7},{7,8},{8,9},{9,10},{10,1... | collective-permute-start | bytes 294920 | tf_op jit(solution)/shard_map/ppermute | solution.py:16
  47.0 7.9 %collective-permute-start.11 = (bf16[192,256]{1,0:T(8,128)(2,1)S(1)}, bf16[192,256]{1,0:T(8,128)(2,1)S(1)}, u32[]{:S(2)}, u32[]{:S(2)}) collective-permute-start(bf16[192,256]{1,0:T(8,128)(2,1)S(1)} %collective-permute-done.9), channel_id=1, source_target_pairs={{0,15},{1,0},{2,1},{3,2},{4,3},{5,4},{6,5},{7,6},{8,7},{9,8},{10,9... | collective-permute-start | bytes 294920 | tf_op jit(solution)/shard_map/ppermute | solution.py:21
  53.0 7.9 %collective-permute-start.10 = (bf16[192,256]{1,0:T(8,128)(2,1)S(1)}, bf16[192,256]{1,0:T(8,128)(2,1)S(1)}, u32[]{:S(2)}, u32[]{:S(2)}) collective-permute-start(bf16[192,256]{1,0:T(8,128)(2,1)S(1)} %collective-permute-done.8), channel_id=1, source_target_pairs={{0,1},{1,2},{2,3},{3,4},{4,5},{5,6},{6,7},{7,8},{8,9},{9,10},{10,1... | collective-permute-start | bytes 294920 | tf_op jit(solution)/shard_map/ppermute | solution.py:16
  55.0 7.9 %collective-permute-start.13 = (bf16[192,256]{1,0:T(8,128)(2,1)S(1)}, bf16[192,256]{1,0:T(8,128)(2,1)S(1)}, u32[]{:S(2)}, u32[]{:S(2)}) collective-permute-start(bf16[192,256]{1,0:T(8,128)(2,1)S(1)} %collective-permute-done.11), channel_id=1, source_target_pairs={{0,15},{1,0},{2,1},{3,2},{4,3},{5,4},{6,5},{7,6},{8,7},{9,8},{10,9... | collective-permute-start | bytes 294920 | tf_op jit(solution)/shard_map/ppermute | solution.py:21
  61.0 7.9 %collective-permute-start.12 = (bf16[192,256]{1,0:T(8,128)(2,1)S(1)}, bf16[192,256]{1,0:T(8,128)(2,1)S(1)}, u32[]{:S(2)}, u32[]{:S(2)}) collective-permute-start(bf16[192,256]{1,0:T(8,128)(2,1)S(1)} %collective-permute-done.10), channel_id=1, source_target_pairs={{0,1},{1,2},{2,3},{3,4},{4,5},{5,6},{6,7},{7,8},{8,9},{9,10},{10,1... | collective-permute-start | bytes 294920 | tf_op jit(solution)/shard_map/ppermute | solution.py:16
  62.9 14.0 %collective-permute-start.15 = (bf16[192,256]{1,0:T(8,128)(2,1)S(1)}, bf16[192,256]{1,0:T(8,128)(2,1)S(1)}, u32[]{:S(2)}, u32[]{:S(2)}) collective-permute-start(bf16[192,256]{1,0:T(8,128)(2,1)S(1)} %collective-permute-done.13), channel_id=1, source_target_pairs={{0,15},{1,0},{2,1},{3,2},{4,3},{5,4},{6,5},{7,6},{8,7},{9,8},{10,9... | collective-permute-start | bytes 294920 | tf_op jit(solution)/shard_map/ppermute | solution.py:21
  68.9 7.9 %collective-permute-start.14 = (bf16[192,256]{1,0:T(8,128)(2,1)S(1)}, bf16[192,256]{1,0:T(8,128)(2,1)S(1)}, u32[]{:S(2)}, u32[]{:S(2)}) collective-permute-start(bf16[192,256]{1,0:T(8,128)(2,1)S(1)} %collective-permute-done.12), channel_id=1, source_target_pairs={{0,1},{1,2},{2,3},{3,4},{4,5},{5,6},{6,7},{7,8},{8,9},{9,10},{10,1... | collective-permute-start | bytes 294920 | tf_op jit(solution)/shard_map/ppermute | solution.py:16
  76.8 7.9 %collective-permute-start.16 = (bf16[192,256]{1,0:T(8,128)(2,1)S(1)}, bf16[192,256]{1,0:T(8,128)(2,1)S(1)}, u32[]{:S(2)}, u32[]{:S(2)}) collective-permute-start(bf16[192,256]{1,0:T(8,128)(2,1)S(1)} %collective-permute-done.14), channel_id=1, source_target_pairs={{0,1},{1,2},{2,3},{3,4},{4,5},{5,6},{6,7},{7,8},{8,9},{9,10},{10,1... | collective-permute-start | bytes 294920 | tf_op jit(solution)/shard_map/ppermute | solution.py:16
Sparse Core Ops, SparseCore 0:
  118.4 71.5 reduce-scatter.1
